TPU v7x, 512 devices: a whole 4x4x16 slice. The times are simulated.
512 devices in a mesh: seq: 64 (over y, z), head: 8 (over x, core).
Axes of the slice: x: 4, y: 4, z: 16, core: 2. Of those that a mesh axis runs over, the one named last changes fastest.
Arguments:
- query_in: bfloat16 [32768, 4096], P('seq', 'head'), may hold values from -128 to 128
- key_in: bfloat16 [32768, 4096], P('seq', 'head'), may hold values from -6 to 6
- value_in: bfloat16 [32768, 4096], P('seq', 'head'), may hold values from -6 to 6
- upstream: bfloat16 [32768, 4096], P('seq', 'head'), may hold values from -24 to 24
- norm_gain: float32 [4096], P('head'), may hold values from 0.1 to 1.9
- state_in: float32 [32, 128, 128], P('head'), may hold values from -96 to 96
Outputs:
- normed_out: bfloat16 [32768, 4096], P('seq', 'head')
- query_grad: bfloat16 [32768, 4096], P('seq', 'head')
- key_grad: bfloat16 [32768, 4096], P('seq', 'head')
- value_grad: bfloat16 [32768, 4096], P('seq', 'head')
- gain_grad: float32 [4096], P('head')
- state_grad: float32 [32, 128, 128], P('head')
All inputs are finite; a program needn't handle non-finite values.
Results may differ from a plain program's by a relative error of at most 0.0026.
Values sent between devices are 32-bit elements; how exact they have to be, the bound alone decides.
A program may use at most 128 MiB of HBM per device.

v0:
```python
import jax
import jax.numpy as jnp
from jax import lax
from jax.sharding import PartitionSpec as P


def entering(x, axis, combine, identity, reverse):
    peers, mine = (lax.axis_size(axis), lax.axis_index(axis))
    everything = lax.all_gather(x, axis)
    start = jnp.broadcast_to(jnp.asarray(identity, x.dtype), x.shape)

    def turn(k, before):
        at = peers - 1 - k if reverse else k
        reached = at > mine if reverse else at < mine
        new = combine(before, everything[at])
        return jnp.where(reached, new, before)

    return lax.fori_loop(0, peers, turn, start)


def add_states(earlier, later):
    return earlier + later


def per_device(query_in, key_in, value_in, upstream, norm_gain, state_in):
    heads_dev = state_in.shape[0]
    head_size = state_in.shape[1]
    count_rows = query_in.shape[0]
    columns_all = heads_dev * head_size * lax.axis_size("head")
    highest = lax.Precision.HIGHEST
    query_heads = query_in.reshape(count_rows, heads_dev, head_size)
    key_heads = key_in.reshape(count_rows, heads_dev, head_size)
    value_heads = value_in.reshape(count_rows, heads_dev, head_size)
    causal = jnp.tril(jnp.ones((count_rows, count_rows), dtype=bool))[None]
    raw_scores = jnp.einsum(
        "thd,shd->hts", query_heads, key_heads, preferred_element_type=jnp.float32
    )
    scores = jnp.where(causal, raw_scores, 0.0).astype(jnp.bfloat16)
    local_kv = jnp.einsum(
        "thd,the->hde", key_heads, value_heads, preferred_element_type=jnp.float32
    )
    earlier_sum = entering(local_kv, "seq", add_states, jnp.zeros_like(local_kv), False)
    running = state_in + earlier_sum
    inside = jnp.einsum("hts,she->the", scores, value_heads, preferred_element_type=jnp.float32)
    carried = jnp.einsum(
        "thd,hde->the", query_heads.astype(jnp.float32), running, precision=highest
    )
    flattened = (inside + carried).reshape(count_rows, heads_dev * head_size)
    upstream_full = upstream.astype(jnp.float32)
    scaled = upstream_full * norm_gain
    squares, products = lax.psum(
        (jnp.sum(flattened * flattened, axis=1), jnp.sum(scaled * flattened, axis=1)), "head"
    )
    inverse = lax.rsqrt(squares / columns_all + 1e-06)[:, None]
    normed = flattened * inverse
    normed_out = (normed * norm_gain).astype(jnp.bfloat16)
    d_full = inverse * (
        scaled - flattened * ((products / columns_all)[:, None] * inverse * inverse)
    )
    gain_part = jnp.sum(upstream_full * normed, axis=0)
    d_low = d_full.astype(jnp.bfloat16).reshape(count_rows, heads_dev, head_size)
    d_heads = d_full.reshape(count_rows, heads_dev, head_size)
    local_qd = jnp.einsum("thd,the->hde", query_heads, d_low, preferred_element_type=jnp.float32)
    later_sum = entering(local_qd, "seq", add_states, jnp.zeros_like(local_qd), True)
    state_grad, gain_grad = lax.psum((local_qd, gain_part), "seq")
    d_raw = jnp.einsum("the,she->hts", d_low, value_heads, preferred_element_type=jnp.float32)
    d_scores = jnp.where(causal, d_raw, 0.0).astype(jnp.bfloat16)
    query_part = jnp.einsum("hts,shd->thd", d_scores, key_heads, preferred_element_type=jnp.float32)
    query_part = query_part + jnp.einsum("the,hde->thd", d_heads, running, precision=highest)
    key_part = jnp.einsum("hts,thd->shd", d_scores, query_heads, preferred_element_type=jnp.float32)
    key_part = key_part + jnp.einsum(
        "she,hde->shd", value_heads.astype(jnp.float32), later_sum, precision=highest
    )
    value_part = jnp.einsum("hts,the->she", scores, d_low, preferred_element_type=jnp.float32)
    value_part = value_part + jnp.einsum(
        "shd,hde->she", key_heads.astype(jnp.float32), later_sum, precision=highest
    )
    flat_shape = (count_rows, heads_dev * head_size)
    return (
        normed_out,
        query_part.astype(jnp.bfloat16).reshape(flat_shape),
        key_part.astype(jnp.bfloat16).reshape(flat_shape),
        value_part.astype(jnp.bfloat16).reshape(flat_shape),
        gain_grad,
        state_grad,
    )


def solution(mesh):
    placed = (
        P("seq", "head"),
        P("seq", "head"),
        P("seq", "head"),
        P("seq", "head"),
        P("head"),
        P("head", None, None),
    )
    return jax.shard_map(
        per_device,
        mesh=mesh,
        in_specs=placed,
        out_specs=(
            P("seq", "head"),
            P("seq", "head"),
            P("seq", "head"),
            P("seq", "head"),
            P("head"),
            P("head", None, None),
        ),
        check_vma=False,
    )
```

profile of v0, /device:TPU:1, one launch (start us, length us, event | category | flops | bytes accessed | tf_op | source)
XLA Modules:
  0.0 847.2 jit_solution(7043653425926259834)
XLA Ops:
  7.2 1.3 copy.115
  8.6 2.0 fusion.18
  11.6 1.3 copy-done.1
  12.9 1.8 convolution_bitcast_fusion.2
  14.7 195.3 %all-gather.5.cloned.1.call-done = f32[256,128,128]{2,1,0:T(8,128)} async-done(((f32[4,128,128]{2,1,0:T(8,128)}), f32[256,128,128]{2,1,0:T(8,128)}) %all-gather.5.cloned.1.call-update) | async-done | bytes 16777232 | tf_op jit(solution)/shard_map/all_gather | solution.py:9
  210.0 68.1 %while.30 = (s32[]{:T(128)}, f32[4,128,128]{2,1,0:T(8,128)S(1)}, s32[]{:T(128)}, f32[64,4,128,128]{3,2,1,0:T(8,128)}, s32[]{:T(128)}, /*index=5*/s32[]{:T(128)}) while((s32[]{:T(128)}, f32[4,128,128]{2,1,0:T(8,128)S(1)}, s32[]{:T(128)}, f32[64,4,128,128]{3,2,1,0:T(8,128)}, s32[]{:T(128)}, /*index=5*/s32[]{:T(128)}) %tuple.91), condition=%wide.region_1.2_spmd.clone, body=%wide.region_0.1_spmd.clone.sunk | while | flops 196612 | bytes 786533 | solution.py:18
  216.4 1.0 add_select_fusion.4
  278.2 3.0 multiply_reduce_fusion
  281.1 12.8 %psum.28 = f32[512]{0:T(512)S(1)} all-reduce(f32[512]{0:T(512)S(1)} %get-tuple-element.264), channel_id=1, replica_groups=mesh['seq'=64,'head'=8] {'head'}, use_global_device_ids=true, to_apply=%region_3.4 | all-reduce | flops 512 | bytes 4096 | tf_op jit(solution)/shard_map/psum | solution.py:51
  294.0 1.6 copy.45
  296.0 14.1 %psum.29 = f32[512]{0:T(512)S(1)} all-reduce(f32[512]{0:T(512)S(1)} %get-tuple-element.244), channel_id=1, replica_groups=mesh['seq'=64,'head'=8] {'head'}, use_global_device_ids=true, to_apply=%region_5.6 | all-reduce | flops 512 | bytes 4096 | tf_op jit(solution)/shard_map/psum | solution.py:51
  310.1 1.7 fusion.13
  311.8 1.3 copy.66
  317.4 1.1 copy-done.8
  318.6 1.9 fusion.3
  320.5 2.0 copy.60
  322.5 112.3 %psum.30 = f32[512]{0:T(512)} all-reduce(f32[512]{0:T(512)S(1)} %get-tuple-element.243), channel_id=1, replica_groups=mesh['seq'=64,'head'=8] {'seq'}, use_global_device_ids=true, to_apply=%region_9.10 | all-reduce | flops 512 | bytes 4096 | tf_op jit(solution)/shard_map/psum | solution.py:65
  434.9 1.4 fusion.36
  437.4 127.3 %all-reduce.2.cloned.1.call-done = f32[4,128,128]{1,2,0:T(8,128)} async-done(((f32[4,128,128]{1,2,0:T(8,128)}), f32[4,128,128]{1,2,0:T(8,128)}) %all-reduce.2.cloned.1.call-update) | async-done | bytes 262160 | tf_op jit(solution)/shard_map/psum | solution.py:65
  564.6 1.9 copy.63
  566.5 199.5 %all-gather.7.cloned.1.call-done = f32[256,128,128]{2,1,0:T(8,128)} async-done(((f32[4,128,128]{2,1,0:T(8,128)}), f32[256,128,128]{2,1,0:T(8,128)}) %all-gather.7.cloned.1.call-update) | async-done | bytes 16777232 | tf_op jit(solution)/shard_map/all_gather | solution.py:9
  766.0 68.4 %while.31 = (s32[]{:T(128)}, f32[4,128,128]{2,1,0:T(8,128)S(1)}, s32[]{:T(128)}, f32[64,4,128,128]{3,2,1,0:T(8,128)}, s32[]{:T(128)}, /*index=5*/s32[]{:T(128)}, s32[]{:T(128)}, s32[]{:T(128)}) while((s32[]{:T(128)}, f32[4,128,128]{2,1,0:T(8,128)S(1)}, s32[]{:T(128)}, f32[64,4,128,128]{3,2,1,0:T(8,128)}, s32[]{:T(128)}, ...), condition=%wide.region_7.8_spmd.clone, body=%wide.region_6.7_spmd.clone.sunk | while | flops 196616 | bytes 786595 | solution.py:18
  834.5 2.5 fusion.5
  837.0 2.0 copy.62
  (182 shorter events, 140.5 us)
Async XLA Ops:
  7.2 3.6 copy-start
  7.2 3.6 copy-start.13
  7.2 202.8 %all-gather.5.cloned.1.call-start = ((), (), s32[]{:S(2)}) async-start(), calls=%async_computation.1 | async-start | bytes 17039360 | tf_op jit(solution)/shard_map/all_gather | solution.py:9
  10.8 0.8 copy-start.15
  10.8 2.1 copy-start.5
  11.5 1.3 copy-start.1
  14.7 263.4 %copy-start.14 = (f32[4,128,128]{2,1,0:T(8,128)S(1)}, f32[4,128,128]{2,1,0:T(8,128)}, u32[]{:S(2)}) copy-start(f32[4,128,128]{2,1,0:T(8,128)} %param.15) | copy-start | bytes 786436
  278.1 15.8 %copy-start.10 = (f32[4,128,128]{2,1,0:T(8,128)}, f32[4,128,128]{2,1,0:T(8,128)S(1)}, u32[]{:S(2)}) copy-start(f32[4,128,128]{2,1,0:T(8,128)S(1)} %add.98) | copy-start | bytes 786436
  278.1 17.4 %copy-start.12 = (bf16[512,512]{1,0:T(8,128)(2,1)S(1)}, bf16[512,512]{1,0:T(8,128)(2,1)}, u32[]{:S(2)}) copy-start(bf16[512,512]{1,0:T(8,128)(2,1)} %param.13) | copy-start | bytes 1572868
  278.2 17.4 %copy-start.17 = (f32[512]{0:T(512)S(1)}, f32[512]{0:T(512)}, u32[]{:S(2)}) copy-start(f32[512]{0:T(512)} %param.14) | copy-start | bytes 6148
  311.8 3.9 copy-start.16
  313.4 0.9 copy-start.9
  314.3 250.4 %all-reduce.2.cloned.1.call-start = ((), (), s32[]{:S(2)}) async-start(), calls=%async_computation | async-start | bytes 524288 | tf_op jit(solution)/shard_map/psum | solution.py:65
  315.0 451.1 %all-gather.7.cloned.1.call-start = ((), (), s32[]{:S(2)}) async-start(), calls=%async_computation.2 | async-start | bytes 17039360 | tf_op jit(solution)/shard_map/all_gather | solution.py:9
  316.6 3.9 copy-start.3
  316.6 2.0 copy-start.8
  316.6 2.0 copy-start.11
  317.4 117.4 %copy-start.2 = (bf16[4,512,512]{2,1,0:T(8,128)(2,1)S(1)}, bf16[4,512,512]{2,1,0:T(8,128)(2,1)}, u32[]{:S(2)}) copy-start(bf16[4,512,512]{2,1,0:T(8,128)(2,1)} %copy-done.1) | copy-start | bytes 6291460
  434.9 2.0 copy-start.4
  564.6 269.8 %copy-start.7 = (f32[4,128,512]{2,1,0:T(8,128)S(1)}, f32[4,128,512]{2,1,0:T(8,128)}, u32[]{:S(2)}) copy-start(f32[4,128,512]{2,1,0:T(8,128)} %fusion.36) | copy-start | bytes 3145732
  834.4 4.6 copy-start.6
Sparse Core Ops, SparseCore 0:
  11.5 198.3 all-gather.4
  318.5 246.0 all-reduce.1
  568.0 197.9 all-gather.6
where the time goes:
time: 852 us; the launch traced here: 847 us
  waiting for transfers between devices  524 us (62%)
  blocking collectives  139 us (16%)
  other arithmetic  135 us (16%)
  matrix products  16.4 us (2%)
  local copies, waits for them, and re-layouts  15.1 us (2%)
  between operations  14 us (2%)
    all_gather x2, waiting for transfers between devices, entering(): everything = lax.all_gather(x, axis)  395 us
    select_n x128, other arithmetic, turn(): return jnp.where(reached, new, before)  133 us
    psum x1, waiting for transfers between devices, per_device(): state_grad, gain_grad = lax.psum((local_qd, gain_part), 'seq')  127 us
    psum x1, blocking collectives, per_device(): state_grad, gain_grad = lax.psum((local_qd, gain_part), 'seq')  112 us
    psum x2, blocking collectives, per_device(): lax.psum((jnp.sum(flattened * flattened, axis=1), jnp.sum(scaled * flatte...  27 us
  transfers between devices with their start and end apart: 3, of which 3 were waited for; matrix products, arithmetic and copies ran while one was open for 1% of the time, Pallas kernels for 0%

commit v1 on v0

v1 whole, which is shorter than its diff:
```python
import functools

import jax
import jax.numpy as jnp
from jax import lax
from jax.experimental import pallas as pl
from jax.experimental.pallas import tpu as pltpu
from jax.sharding import PartitionSpec as P

F32 = jnp.float32
BF16 = jnp.bfloat16
MESH = pl.DeviceIdType.MESH
HEAD = 128
ROWS = 8
PLANES = 16
LINES = 4


def nn(a, b):
    return lax.dot_general(a, b, (((1,), (0,)), ((), ())), preferred_element_type=F32)


def nt(a, b):
    return lax.dot_general(a, b, (((1,), (1,)), ((), ())), preferred_element_type=F32)


def tn(a, b):
    return lax.dot_general(a, b, (((0,), (0,)), ((), ())), preferred_element_type=F32)


def halves(x):
    high = x.astype(BF16)
    return high, (x - high.astype(F32)).astype(BF16)


def copy_to(src, dst, send, recv, **where):
    return pltpu.make_async_remote_copy(
        src, dst, send, recv, device_id=where, device_id_type=MESH
    )


def kernel(
    q_in, k_in, v_in, u_in, gain_ref, state_ref,
    normed_out, qgrad_out, kgrad_out, vgrad_out, gain_out, state_out,
    q, k, v, u, qt, att, dfull, dlow, kpart, vpart,
    normed_buf, qgrad_buf, kgrad_buf, vgrad_buf,
    local1, got1, part1, before, local2, got2, part2, after,
    stats, own_row, rows,
    in_sem, out_sem, send_sem, recv_sem,
):
    n_seq = lax.axis_size("seq")
    n_head = lax.axis_size("head")
    me = lax.axis_index("seq")
    mine = lax.axis_index("head")
    plane = lax.rem(me, PLANES)
    line = me // PLANES
    tokens = q.shape[0]
    heads = q.shape[1] // HEAD
    half = tokens // 2

    loads = [
        pltpu.make_async_copy(src, dst, in_sem.at[i])
        for i, (src, dst) in enumerate(((k_in, k), (v_in, v), (q_in, q), (u_in, u)))
    ]
    for load in loads:
        load.start()

    def step_z(j):
        far = (j + 1) // 2
        away = PLANES // 2 + jnp.where(lax.rem(j, 2) == 1, -far, far)
        return lax.rem(plane + away, PLANES)

    def each_seq(act):
        def body(j, carry):
            z = step_z(j)
            for dy in (2, 1, 3, 0):
                act(lax.rem(line + dy, LINES) * PLANES + z)
            return carry

        lax.fori_loop(0, PLANES - 1, body, 0)
        for dy in (2, 1, 3):
            act(lax.rem(line + dy, LINES) * PLANES + plane)

    barrier = pltpu.get_barrier_semaphore()
    each_seq(
        lambda d: pl.semaphore_signal(barrier, inc=1, device_id={"seq": d}, device_id_type=MESH)
    )
    for i in range(1, n_head):
        pl.semaphore_signal(
            barrier, inc=1, device_id={"head": lax.rem(mine + i, n_head)}, device_id_type=MESH
        )

    def cols(h):
        return slice(h * HEAD, (h + 1) * HEAD)

    def lower(x):
        r = lax.broadcasted_iota(jnp.int32, x.shape, 0)
        c = lax.broadcasted_iota(jnp.int32, x.shape, 1)
        return r >= c

    def upper(x):
        r = lax.broadcasted_iota(jnp.int32, x.shape, 0)
        c = lax.broadcasted_iota(jnp.int32, x.shape, 1)
        return r <= c

    lo, hi = slice(0, half), slice(half, tokens)

    def causal(a, b, c):
        s = nt(a[lo], b[lo])
        top = nn(jnp.where(lower(s), s, 0.0).astype(BF16), c[lo])
        s = nt(a[hi], b[hi])
        low = nn(jnp.where(lower(s), s, 0.0).astype(BF16), c[hi])
        low = low + nn(nt(a[hi], b[lo]).astype(BF16), c[lo])
        return top, low

    def anticausal(a, b, c):
        s = nt(a[hi], b[hi])
        low = nn(jnp.where(upper(s), s, 0.0).astype(BF16), c[hi])
        s = nt(a[lo], b[lo])
        top = nn(jnp.where(upper(s), s, 0.0).astype(BF16), c[lo])
        top = top + nn(nt(a[lo], b[hi]).astype(BF16), c[hi])
        return top, low

    loads[0].wait()
    loads[1].wait()
    for h in range(heads):
        kv = tn(k[:, cols(h)], v[:, cols(h)])
        local1[h * PLANES : (h + 1) * PLANES] = kv.reshape(PLANES, ROWS, HEAD)
    loads[2].wait()
    loads[3].wait()

    def forward_inside(h):
        top, low = causal(q[:, cols(h)], k[:, cols(h)], v[:, cols(h)])
        att[lo, cols(h)] = top
        att[hi, cols(h)] = low

    forward_inside(0)
    pl.semaphore_wait(barrier, n_seq - 1 + n_head - 1)

    def all_but_one(ref):
        return ref.at[pl.ds(0, n_seq - 1)]

    def scatter(local, got, sems):
        each_seq(
            lambda d: copy_to(
                local.at[d], got.at[me], send_sem.at[sems], recv_sem.at[sems], seq=d
            ).start()
        )
        got[me] = local[me]

    def arrived(ref, sems):
        ref = all_but_one(ref)
        copy_to(ref, ref, send_sem.at[sems], recv_sem.at[sems], seq=me).wait_recv()

    def sent(ref, sems):
        ref = all_but_one(ref)
        copy_to(ref, ref, send_sem.at[sems], recv_sem.at[sems], seq=me).wait_send()

    scatter(local1, got1, 0)
    forward_inside(1)
    for h in range(heads):
        qt[h] = q[:, cols(h)].T
    arrived(got1, 0)
    total = state_ref[me]
    for b in range(n_seq):
        part1[b] = total
        total = total + got1[b]
    scatter(part1, before, 1)
    for h in range(2, heads):
        forward_inside(h)
    arrived(before, 1)

    def state_of(ref, h):
        return ref[h * PLANES : (h + 1) * PLANES].reshape(HEAD, HEAD)

    def gain_of(h):
        return gain_ref[h : h + 1, :]

    squares = jnp.zeros((tokens, HEAD), F32)
    products = jnp.zeros((tokens, HEAD), F32)
    for h in range(heads):
        high, low = halves(state_of(before, h))
        qh = q[:, cols(h)]
        a = att[:, cols(h)] + (nn(qh, high) + nn(qh, low))
        att[:, cols(h)] = a
        squares = squares + a * a
        products = products + a * (u[:, cols(h)].astype(F32) * gain_of(h))
    blocks = tokens // HEAD
    for j in range(blocks):
        rows_j = slice(j * HEAD, (j + 1) * HEAD)
        stats[mine, j : j + 1, :] = jnp.sum(squares[rows_j].T, axis=0, keepdims=True)
        stats[mine, blocks + j : blocks + j + 1, :] = jnp.sum(
            products[rows_j].T, axis=0, keepdims=True
        )
    for i in range(1, n_head):
        copy_to(
            stats.at[mine], stats.at[mine], send_sem.at[2], recv_sem.at[2],
            head=lax.rem(mine + i, n_head),
        ).start()
    others = stats.at[pl.ds(0, n_head - 1)]
    copy_to(others, others, send_sem.at[2], recv_sem.at[2], head=mine).wait_recv()
    total = stats[0]
    for i in range(1, n_head):
        total = total + stats[i]
    mean = total * (1.0 / (heads * HEAD * n_head))
    inverse = lax.rsqrt(mean[:blocks] + 1e-06)
    coef = mean[blocks:] * inverse * inverse

    def column(x, j):
        return jnp.broadcast_to(x[j : j + 1, :], (HEAD, HEAD)).T

    inverse = jnp.concatenate([column(inverse, j) for j in range(blocks)], axis=0)
    coef = jnp.concatenate([column(coef, j) for j in range(blocks)], axis=0)
    for h in range(heads):
        scaled = u[:, cols(h)].astype(F32) * gain_of(h)
        d = inverse * (scaled - att[:, cols(h)] * coef)
        d_low = d.astype(BF16)
        dfull[:, cols(h)] = d
        dlow[:, cols(h)] = d_low
        local2[h * PLANES : (h + 1) * PLANES] = nn(qt[h], d_low).reshape(PLANES, ROWS, HEAD)
    scatter(local2, got2, 3)

    own_row[1] = jnp.zeros((ROWS, HEAD), F32)
    for h in range(heads):
        normed = att[:, cols(h)] * inverse
        normed_buf[:, cols(h)] = (normed * gain_of(h)).astype(BF16)
        own_row[1, h : h + 1, :] = jnp.sum(
            u[:, cols(h)].astype(F32) * normed, axis=0, keepdims=True
        )
    stores = [pltpu.make_async_copy(normed_buf, normed_out, out_sem.at[0])]
    stores[0].start()

    def query_gradient(h):
        d_low = dlow[:, cols(h)]
        d_rest = (dfull[:, cols(h)] - d_low.astype(F32)).astype(BF16)
        high, low = halves(state_of(before, h))
        carried = nt(d_low, high) + (nt(d_low, low) + nt(d_rest, high))
        top, low = causal(d_low, v[:, cols(h)], k[:, cols(h)])
        qgrad_buf[lo, cols(h)] = (top + carried[lo]).astype(BF16)
        qgrad_buf[hi, cols(h)] = (low + carried[hi]).astype(BF16)

    for h in range(heads):
        query_gradient(h)
    stores.append(pltpu.make_async_copy(qgrad_buf, qgrad_out, out_sem.at[1]))
    stores[1].start()

    arrived(got2, 3)
    total = jnp.zeros((ROWS, HEAD), F32)
    for b in reversed(range(n_seq)):
        part2[b] = total
        total = total + got2[b]
    own_row[0] = total
    scatter(part2, after, 4)

    def along_z(j):
        far = (j + 1) // 2
        return step_z(j)

    def send_row(j, carry):
        z = step_z(j)
        copy_to(
            own_row, rows.at[line, pl.ds(2 * plane, 2)], send_sem.at[5], recv_sem.at[5],
            seq=line * PLANES + z,
        ).start()
        return carry

    lax.fori_loop(0, PLANES - 1, send_row, 0)
    rows[line, pl.ds(2 * plane, 2)] = own_row[...]

    for h in range(heads):
        top, low = anticausal(v[:, cols(h)], dlow[:, cols(h)], q[:, cols(h)])
        kpart[lo, cols(h)] = top
        kpart[hi, cols(h)] = low
        top, low = anticausal(k[:, cols(h)], q[:, cols(h)], dlow[:, cols(h)])
        vpart[lo, cols(h)] = top
        vpart[hi, cols(h)] = low

    some = rows.at[0, pl.ds(0, 2 * (PLANES - 1))]
    copy_to(some, some, send_sem.at[5], recv_sem.at[5], seq=me).wait_recv()
    for i in (2, 1, 3):
        copy_to(
            rows.at[line], rows.at[line], send_sem.at[6], recv_sem.at[6],
            seq=lax.rem(line + i, LINES) * PLANES + plane,
        ).start()

    arrived(after, 4)
    for h in range(heads):
        high, low = halves(state_of(after, h))
        vh, kh = v[:, cols(h)], k[:, cols(h)]
        kgrad_buf[:, cols(h)] = (kpart[:, cols(h)] + (nt(vh, high) + nt(vh, low))).astype(BF16)
        vgrad_buf[:, cols(h)] = (vpart[:, cols(h)] + (nn(kh, high) + nn(kh, low))).astype(BF16)
    stores.append(pltpu.make_async_copy(kgrad_buf, kgrad_out, out_sem.at[2]))
    stores.append(pltpu.make_async_copy(vgrad_buf, vgrad_out, out_sem.at[3]))
    stores[2].start()
    stores[3].start()

    some = rows.at[pl.ds(0, LINES - 1)]
    copy_to(some, some, send_sem.at[6], recv_sem.at[6], seq=me).wait_recv()
    gain = jnp.zeros((ROWS, HEAD), F32)
    for y in range(LINES):
        for z in range(PLANES):
            state_out[y * PLANES + z] = rows[y, 2 * z]
            gain = gain + rows[y, 2 * z + 1]
    gain_out[...] = gain[:heads]

    for store in stores:
        store.wait()
    sent(local1, 0)
    sent(part1, 1)
    copy_to(others, others, send_sem.at[2], recv_sem.at[2], head=mine).wait_send()
    sent(local2, 3)
    sent(part2, 4)
    some = rows.at[0, pl.ds(0, 2 * (PLANES - 1))]
    copy_to(some, some, send_sem.at[5], recv_sem.at[5], seq=me).wait_send()
    some = rows.at[pl.ds(0, LINES - 1)]
    copy_to(some, some, send_sem.at[6], recv_sem.at[6], seq=me).wait_send()


def per_device(query_in, key_in, value_in, upstream, norm_gain, state_in):
    tokens, columns = query_in.shape
    heads = state_in.shape[0]
    n_seq = lax.axis_size("seq")
    n_head = lax.axis_size("head")
    wide = jax.ShapeDtypeStruct((tokens, columns), BF16)
    slices = (n_seq, ROWS, HEAD)
    vmem = pl.BlockSpec(memory_space=pltpu.VMEM)
    anywhere = pl.BlockSpec(memory_space=pl.ANY)
    low = pltpu.VMEM((tokens, columns), BF16)
    full = pltpu.VMEM((tokens, columns), F32)
    outs = pl.pallas_call(
        kernel,
        name="attention_and_gradients",
        out_shape=(
            wide, wide, wide, wide,
            jax.ShapeDtypeStruct((heads, HEAD), F32),
            jax.ShapeDtypeStruct(slices, F32),
        ),
        in_specs=[anywhere] * 4 + [vmem] * 2,
        out_specs=[anywhere] * 4 + [vmem] * 2,
        scratch_shapes=[low] * 4
        + [pltpu.VMEM((heads, HEAD, tokens), BF16), full, full, low, full, full]
        + [low] * 4
        + [pltpu.VMEM(slices, F32)] * 8
        + [
            pltpu.VMEM((n_head, ROWS, HEAD), F32),
            pltpu.VMEM((2, ROWS, HEAD), F32),
            pltpu.VMEM((LINES, 2 * PLANES, ROWS, HEAD), F32),
            pltpu.SemaphoreType.DMA((4,)),
            pltpu.SemaphoreType.DMA((4,)),
            pltpu.SemaphoreType.DMA((7,)),
            pltpu.SemaphoreType.DMA((7,)),
        ],
        compiler_params=pltpu.CompilerParams(
            collective_id=0, has_side_effects=True, vmem_limit_bytes=40 << 20
        ),
    )(
        query_in, key_in, value_in, upstream,
        norm_gain.reshape(heads, HEAD), state_in.reshape(slices),
    )
    return (
        outs[0], outs[1], outs[2], outs[3],
        outs[4].reshape(heads * HEAD), outs[5].reshape(state_in.shape),
    )


def solution(mesh):
    wide = P("seq", "head")
    return jax.shard_map(
        per_device,
        mesh=mesh,
        in_specs=(wide, wide, wide, wide, P("head"), P("head", None, None)),
        out_specs=(wide, wide, wide, wide, P("head"), P("head", None, None)),
        check_vma=False,
    )
```

time: 852 us -> 106 us (0.12)
  waiting for transfers between devices: 524 us -> 0 us
  blocking collectives: 139 us -> 0 us
  other arithmetic: 135 us -> 0 us
  Pallas kernels: 0 us -> 94.3 us
  matrix products: 16.4 us -> 0 us
  between operations: 14 us -> 0.66 us
    all_gather x2 -> x0, waiting for transfers between devices: 395 us -> none  [entering(): everything = lax.all_gather(x, axis)]
    psum x3 -> x0, blocking collectives: 139 us -> none  [the longest x1 112 us: per_device(): state_grad, gain_grad = lax.psum((local_qd, gain_part), 'seq')]
    select_n x128 -> x0, other arithmetic: 133 us -> none  [turn(): return jnp.where(reached, new, before)]
    psum x1 -> x0, waiting for transfers between devices: 127 us -> none  [per_device(): state_grad, gain_grad = lax.psum((local_qd, gain_part), 'seq')]
    pallas_call x0 -> x1, Pallas kernels: none -> 94.3 us  [per_device(): pl.pallas_call(kernel, name='attention_and_gradients', out_shape=(wide, w...]
    dot_general x12 -> x0, matrix products: 16.4 us -> none  [the longest x1 2.97 us: per_device(): jnp.einsum('thd,hde->the', query_heads.astype(jnp.float32), running, prec...]
  transfers between devices with their start and end apart: 3 -> 0, of which waited for: 3 -> 0; matrix products, arithmetic and copies ran while one was open for 1% -> 0% of each run, Pallas kernels for 0% -> 0%
where the time goes in v1:
time: 106 us; the launch traced here: 105 us
  Pallas kernels  94.3 us (89%)
  local copies, waits for them, and re-layouts  10.2 us (10%)
    pallas_call x1, Pallas kernels, per_device(): pl.pallas_call(kernel, name='attention_and_gradients', out_shape=(wide, w...  94.3 us
    unnamed x18, local copies, waits for them, and re-layouts  10.2 us

profile of v1, /device:TPU:1, one launch (start us, length us, event | category | flops | bytes accessed | tf_op | source)
XLA Modules:
  0.0 105.2 jit_solution(12693929431357967813)
XLA Ops:
  0.6 0.0 copy-start.5
  0.6 0.7 copy-done.5
  1.3 0.0 copy-start
  1.3 1.0 copy-done
  2.4 0.0 copy-start.1
  2.4 1.0 copy-done.1
  3.4 0.0 copy-start.2
  3.4 1.0 copy-done.2
  4.4 0.0 copy-start.3
  4.4 1.0 copy-done.3
  5.5 0.0 copy-start.4
  5.5 0.9 copy-done.4
  6.4 94.3 %attention_and_gradients.1 = (bf16[512,512]{1,0:T(8,128)(2,1)S(1)}, bf16[512,512]{1,0:T(8,128)(2,1)S(1)}, bf16[512,512]{1,0:T(8,128)(2,1)S(1)}, bf16[512,512]{1,...) custom-call(bf16[512,512]{1,0:T(8,128)(2,1)S(1)} %copy-done, bf16[512,512]{1,0:T(8,128)(2,1)S(1)} %copy-done.1, ...), custom_call_target="tpu_custom_call" | custom-call | tf_op jit(solution)/shard_map/attention_and_gradients/pallas_call | solution.py:330
  100.7 0.8 copy.18
  101.5 0.8 copy.19
  102.3 0.8 copy.20
  103.1 0.8 copy.21
  103.9 0.6 copy.22
  104.5 0.7 copy.23
Async XLA Ops:
  0.6 0.7 copy-start.5
  1.3 1.0 copy-start
  2.4 1.0 copy-start.1
  3.4 1.0 copy-start.2
  4.4 1.0 copy-start.3
  5.5 0.9 copy-start.4

commit v2 on v1

--- a/solution.py
+++ b/solution.py
@@ -40,13 +40,12 @@
 
 
 def kernel(
-    q_in, k_in, v_in, u_in, gain_ref, state_ref,
+    q_in, k_in, v_in, u_in, gain_in, state_in,
     normed_out, qgrad_out, kgrad_out, vgrad_out, gain_out, state_out,
-    q, k, v, u, qt, att, dfull, dlow, kpart, vpart,
-    normed_buf, qgrad_buf, kgrad_buf, vgrad_buf,
+    q, k, v, u, gain_ref, state_ref, qt, att, dfull, dlow, kpart, vpart,
     local1, got1, part1, before, local2, got2, part2, after,
-    stats, own_row, rows,
-    in_sem, out_sem, send_sem, recv_sem,
+    stats, totals, gains, gains_got,
+    in_sem, send_sem, recv_sem,
 ):
     n_seq = lax.axis_size("seq")
     n_head = lax.axis_size("head")
@@ -60,7 +59,12 @@
 
     loads = [
         pltpu.make_async_copy(src, dst, in_sem.at[i])
-        for i, (src, dst) in enumerate(((k_in, k), (v_in, v), (q_in, q), (u_in, u)))
+        for i, (src, dst) in enumerate(
+            (
+                (k_in, k), (v_in, v), (q_in, q),
+                (u_in, u), (gain_in, gain_ref), (state_in, state_ref),
+            )
+        )
     ]
     for load in loads:
         load.start()
@@ -126,8 +130,8 @@
     for h in range(heads):
         kv = tn(k[:, cols(h)], v[:, cols(h)])
         local1[h * PLANES : (h + 1) * PLANES] = kv.reshape(PLANES, ROWS, HEAD)
-    loads[2].wait()
-    loads[3].wait()
+    for load in loads[2:]:
+        load.wait()
 
     def forward_inside(h):
         top, low = causal(q[:, cols(h)], k[:, cols(h)], v[:, cols(h)])
@@ -220,15 +224,32 @@
         local2[h * PLANES : (h + 1) * PLANES] = nn(qt[h], d_low).reshape(PLANES, ROWS, HEAD)
     scatter(local2, got2, 3)
 
-    own_row[1] = jnp.zeros((ROWS, HEAD), F32)
+    gains[0] = jnp.zeros((ROWS, HEAD), F32)
     for h in range(heads):
         normed = att[:, cols(h)] * inverse
-        normed_buf[:, cols(h)] = (normed * gain_of(h)).astype(BF16)
-        own_row[1, h : h + 1, :] = jnp.sum(
+        normed_out[:, cols(h)] = (normed * gain_of(h)).astype(BF16)
+        gains[0, h : h + 1, :] = jnp.sum(
             u[:, cols(h)].astype(F32) * normed, axis=0, keepdims=True
         )
-    stores = [pltpu.make_async_copy(normed_buf, normed_out, out_sem.at[0])]
-    stores[0].start()
+
+    def partner(i):
+        step = (1, 2, 4, 8, 1, 2)[i]
+        near = plane if i < 4 else line
+        other = near + step - 2 * step * lax.rem(near // step, 2)
+        return line * PLANES + other if i < 4 else other * PLANES + plane
+
+    def gain_copy(i):
+        return copy_to(
+            gains.at[i], gains_got.at[i], send_sem.at[7 + i], recv_sem.at[7 + i], seq=partner(i)
+        )
+
+    def gain_step(i):
+        gain_copy(i).wait_recv()
+        gains[i + 1] = gains[i] + gains_got[i]
+        if i < 5:
+            gain_copy(i + 1).start()
+
+    gain_copy(0).start()
 
     def query_gradient(h):
         d_low = dlow[:, cols(h)]
@@ -236,36 +257,31 @@
         high, low = halves(state_of(before, h))
         carried = nt(d_low, high) + (nt(d_low, low) + nt(d_rest, high))
         top, low = causal(d_low, v[:, cols(h)], k[:, cols(h)])
-        qgrad_buf[lo, cols(h)] = (top + carried[lo]).astype(BF16)
-        qgrad_buf[hi, cols(h)] = (low + carried[hi]).astype(BF16)
+        qgrad_out[lo, cols(h)] = (top + carried[lo]).astype(BF16)
+        qgrad_out[hi, cols(h)] = (low + carried[hi]).astype(BF16)
 
     for h in range(heads):
         query_gradient(h)
-    stores.append(pltpu.make_async_copy(qgrad_buf, qgrad_out, out_sem.at[1]))
-    stores[1].start()
+        if h == 1:
+            gain_step(0)
+    gain_step(1)
 
     arrived(got2, 3)
     total = jnp.zeros((ROWS, HEAD), F32)
     for b in reversed(range(n_seq)):
         part2[b] = total
         total = total + got2[b]
-    own_row[0] = total
-    scatter(part2, after, 4)
-
-    def along_z(j):
-        far = (j + 1) // 2
-        return step_z(j)
-
-    def send_row(j, carry):
-        z = step_z(j)
+    totals[me] = total
+
+    def send_total(j, carry):
         copy_to(
-            own_row, rows.at[line, pl.ds(2 * plane, 2)], send_sem.at[5], recv_sem.at[5],
-            seq=line * PLANES + z,
+            totals.at[me], totals.at[me], send_sem.at[5], recv_sem.at[5],
+            seq=line * PLANES + step_z(j),
         ).start()
         return carry
 
-    lax.fori_loop(0, PLANES - 1, send_row, 0)
-    rows[line, pl.ds(2 * plane, 2)] = own_row[...]
+    lax.fori_loop(0, PLANES - 1, send_total, 0)
+    scatter(part2, after, 4)
 
     for h in range(heads):
         top, low = anticausal(v[:, cols(h)], dlow[:, cols(h)], q[:, cols(h)])
@@ -275,45 +291,49 @@
         vpart[lo, cols(h)] = top
         vpart[hi, cols(h)] = low
 
-    some = rows.at[0, pl.ds(0, 2 * (PLANES - 1))]
+    row = totals.at[pl.ds(line * PLANES, PLANES)]
+    some = totals.at[pl.ds(0, PLANES - 1)]
     copy_to(some, some, send_sem.at[5], recv_sem.at[5], seq=me).wait_recv()
     for i in (2, 1, 3):
         copy_to(
-            rows.at[line], rows.at[line], send_sem.at[6], recv_sem.at[6],
+            row, row, send_sem.at[6], recv_sem.at[6],
             seq=lax.rem(line + i, LINES) * PLANES + plane,
         ).start()
+    gain_step(2)
 
     arrived(after, 4)
     for h in range(heads):
         high, low = halves(state_of(after, h))
         vh, kh = v[:, cols(h)], k[:, cols(h)]
-        kgrad_buf[:, cols(h)] = (kpart[:, cols(h)] + (nt(vh, high) + nt(vh, low))).astype(BF16)
-        vgrad_buf[:, cols(h)] = (vpart[:, cols(h)] + (nn(kh, high) + nn(kh, low))).astype(BF16)
-    stores.append(pltpu.make_async_copy(kgrad_buf, kgrad_out, out_sem.at[2]))
-    stores.append(pltpu.make_async_copy(vgrad_buf, vgrad_out, out_sem.at[3]))
-    stores[2].start()
-    stores[3].start()
-
-    some = rows.at[pl.ds(0, LINES - 1)]
-    copy_to(some, some, send_sem.at[6], recv_sem.at[6], seq=me).wait_recv()
-    gain = jnp.zeros((ROWS, HEAD), F32)
-    for y in range(LINES):
-        for z in range(PLANES):
-            state_out[y * PLANES + z] = rows[y, 2 * z]
-            gain = gain + rows[y, 2 * z + 1]
-    gain_out[...] = gain[:heads]
-
-    for store in stores:
-        store.wait()
+        kgrad_out[:, cols(h)] = (kpart[:, cols(h)] + (nt(vh, high) + nt(vh, low))).astype(BF16)
+        vgrad_out[:, cols(h)] = (vpart[:, cols(h)] + (nn(kh, high) + nn(kh, low))).astype(BF16)
+
+    gain_step(3)
+    three = totals.at[pl.ds(0, (LINES - 1) * PLANES)]
+    copy_to(three, three, send_sem.at[6], recv_sem.at[6], seq=me).wait_recv()
+    state_out[...] = totals[...]
+    gain_step(4)
+    gain_step(5)
+    gain_out[...] = gains[6, :heads, :]
+
     sent(local1, 0)
     sent(part1, 1)
     copy_to(others, others, send_sem.at[2], recv_sem.at[2], head=mine).wait_send()
     sent(local2, 3)
     sent(part2, 4)
-    some = rows.at[0, pl.ds(0, 2 * (PLANES - 1))]
     copy_to(some, some, send_sem.at[5], recv_sem.at[5], seq=me).wait_send()
-    some = rows.at[pl.ds(0, LINES - 1)]
-    copy_to(some, some, send_sem.at[6], recv_sem.at[6], seq=me).wait_send()
+    copy_to(three, three, send_sem.at[6], recv_sem.at[6], seq=me).wait_send()
+    for i in range(6):
+        gain_copy(i).wait_send()
+
+
+def store_kernel(*refs):
+    n = len(refs) // 2
+    stores = [pltpu.make_async_copy(refs[i], refs[n + i], refs[-1].at[i]) for i in range(n)]
+    for store in stores:
+        store.start()
+    for store in stores:
+        store.wait()
 
 
 def per_device(query_in, key_in, value_in, upstream, norm_gain, state_in):
@@ -325,38 +345,49 @@
     slices = (n_seq, ROWS, HEAD)
     vmem = pl.BlockSpec(memory_space=pltpu.VMEM)
     anywhere = pl.BlockSpec(memory_space=pl.ANY)
+    hbm = pl.BlockSpec(memory_space=pltpu.HBM)
     low = pltpu.VMEM((tokens, columns), BF16)
     full = pltpu.VMEM((tokens, columns), F32)
+    shapes = (
+        wide, wide, wide, wide,
+        jax.ShapeDtypeStruct((heads, HEAD), F32),
+        jax.ShapeDtypeStruct(slices, F32),
+    )
     outs = pl.pallas_call(
         kernel,
         name="attention_and_gradients",
-        out_shape=(
-            wide, wide, wide, wide,
-            jax.ShapeDtypeStruct((heads, HEAD), F32),
-            jax.ShapeDtypeStruct(slices, F32),
-        ),
-        in_specs=[anywhere] * 4 + [vmem] * 2,
-        out_specs=[anywhere] * 4 + [vmem] * 2,
+        out_shape=shapes,
+        in_specs=[hbm] * 6,
+        out_specs=[vmem] * 6,
         scratch_shapes=[low] * 4
+        + [pltpu.VMEM((heads, HEAD), F32), pltpu.VMEM(slices, F32)]
         + [pltpu.VMEM((heads, HEAD, tokens), BF16), full, full, low, full, full]
-        + [low] * 4
         + [pltpu.VMEM(slices, F32)] * 8
         + [
             pltpu.VMEM((n_head, ROWS, HEAD), F32),
-            pltpu.VMEM((2, ROWS, HEAD), F32),
-            pltpu.VMEM((LINES, 2 * PLANES, ROWS, HEAD), F32),
-            pltpu.SemaphoreType.DMA((4,)),
-            pltpu.SemaphoreType.DMA((4,)),
-            pltpu.SemaphoreType.DMA((7,)),
-            pltpu.SemaphoreType.DMA((7,)),
+            pltpu.VMEM(slices, F32),
+            pltpu.VMEM((7, ROWS, HEAD), F32),
+            pltpu.VMEM((6, ROWS, HEAD), F32),
+            pltpu.SemaphoreType.DMA((6,)),
+            pltpu.SemaphoreType.DMA((13,)),
+            pltpu.SemaphoreType.DMA((13,)),
         ],
         compiler_params=pltpu.CompilerParams(
-            collective_id=0, has_side_effects=True, vmem_limit_bytes=40 << 20
+            collective_id=0, has_side_effects=True, vmem_limit_bytes=51 << 20
         ),
     )(
         query_in, key_in, value_in, upstream,
         norm_gain.reshape(heads, HEAD), state_in.reshape(slices),
     )
+    outs = pl.pallas_call(
+        store_kernel,
+        name="store",
+        out_shape=shapes,
+        in_specs=[anywhere] * 6,
+        out_specs=[hbm] * 6,
+        scratch_shapes=[pltpu.SemaphoreType.DMA((6,))],
+        compiler_params=pltpu.CompilerParams(vmem_limit_bytes=1 << 20),
+    )(*outs)
     return (
         outs[0], outs[1], outs[2], outs[3],
         outs[4].reshape(heads * HEAD), outs[5].reshape(state_in.shape),

time: 106 us -> 94.9 us (0.90)
  the two profiles are of different devices: /device:TPU:1 before, /device:TPU:2 now
where the time goes in v2:
time: 94.9 us; the launch traced here: 94.7 us
  Pallas kernels  92.5 us (97%)
  local copies, waits for them, and re-layouts  1.62 us (2%)
    pallas_call x1, Pallas kernels, per_device(): pl.pallas_call(kernel, name='attention_and_gradients', out_shape=shapes,...  91 us

profile of v2, /device:TPU:2, one launch (start us, length us, event | category | flops | bytes accessed | tf_op | source)
XLA Modules:
  0.0 94.7 jit_solution(2468954381527132967)
XLA Ops:
  0.6 0.0 copy-start.1
  0.6 0.7 copy-done.1
  1.3 0.0 copy-start
  1.3 0.9 %copy-done = f32[4,128,128]{2,1,0:T(8,128)S(1)} copy-done((f32[4,128,128]{2,1,0:T(8,128)S(1)}, f32[4,128,128]{2,1,0:T(8,128)}, u32[]{:S(2)}) %copy-start) | copy-done | bytes 262168
  2.3 91.0 %attention_and_gradients.1 = (bf16[512,512]{1,0:T(8,128)(2,1)S(1)}, bf16[512,512]{1,0:T(8,128)(2,1)S(1)}, bf16[512,512]{1,0:T(8,128)(2,1)S(1)}, bf16[512,512]{1,...) custom-call(bf16[512,512]{1,0:T(8,128)(2,1)} %q_in.1, bf16[512,512]{1,0:T(8,128)(2,1)} %k_in.1, ...), custom_call_target="tpu_custom_call" | custom-call | tf_op jit(solution)/shard_map/attention_and_gradients/pallas_call | solution.py:356
  93.3 1.5 %store.1 = (bf16[512,512]{1,0:T(8,128)(2,1)}, bf16[512,512]{1,0:T(8,128)(2,1)}, bf16[512,512]{1,0:T(8,128)(2,1)}, bf16[512,512]{1,0:T(8,128)(2,1)}, f32[4,128]{1,0:T(4,128)}, /*index=5*/f32[64,8,128]{2,1,0:T(8,128)}) custom-call(bf16[512,512]{1,0:T(8,128)(2,1)S(1)} %get-tuple-element.18.refs_0_, bf16[512,512]{1,0:T(8,128)(2,1)S(1)} %get-tuple-element.19.refs_1_, ...), custom_call_target="tpu_custom_call" | custom-call | tf_op jit(solution)/shard_map/store/pallas_call | solution.py:382
Async XLA Ops:
  0.6 0.7 copy-start.1
  1.3 0.9 %copy-start = (f32[4,128,128]{2,1,0:T(8,128)S(1)}, f32[4,128,128]{2,1,0:T(8,128)}, u32[]{:S(2)}) copy-start(f32[4,128,128]{2,1,0:T(8,128)} %param.11) | copy-start | bytes 786436

commit v3 on v2

--- a/solution.py
+++ b/solution.py
@@ -43,9 +43,10 @@
     q_in, k_in, v_in, u_in, gain_in, state_in,
     normed_out, qgrad_out, kgrad_out, vgrad_out, gain_out, state_out,
     q, k, v, u, gain_ref, state_ref, qt, att, dfull, dlow, kpart, vpart,
-    local1, got1, part1, before, local2, got2, part2, after,
+    local1, before, mate1, sums1, got1, part1, back1, share1,
+    local2, after, mate2, sums2, got2, part2, back2, share2,
     stats, totals, gains, gains_got,
-    in_sem, send_sem, recv_sem,
+    in_sem, send_sem, recv_sem, scan_send, scan_recv,
 ):
     n_seq = lax.axis_size("seq")
     n_head = lax.axis_size("head")
@@ -74,21 +75,35 @@
         away = PLANES // 2 + jnp.where(lax.rem(j, 2) == 1, -far, far)
         return lax.rem(plane + away, PLANES)
 
-    def each_seq(act):
-        def body(j, carry):
-            z = step_z(j)
-            for dy in (2, 1, 3, 0):
-                act(lax.rem(line + dy, LINES) * PLANES + z)
-            return carry
-
-        lax.fori_loop(0, PLANES - 1, body, 0)
-        for dy in (2, 1, 3):
-            act(lax.rem(line + dy, LINES) * PLANES + plane)
+    pair, side = plane // 2, lax.rem(plane, 2)
+    pairs = PLANES // 2
+    mate = line * PLANES + 2 * pair + 1 - side
+    away = [pairs // 2]
+    for far in range(1, pairs // 2 + 1):
+        away += [pairs // 2 - far, pairs // 2 + far]
+    away = away[:pairs]
+
+    def pair_at(offset):
+        return lax.rem(pair + offset, pairs)
+
+    def line_at(offset):
+        return lax.rem(line + offset, LINES)
+
+    def device(y, p, at_side):
+        return y * PLANES + 2 * p + at_side
 
     barrier = pltpu.get_barrier_semaphore()
-    each_seq(
-        lambda d: pl.semaphore_signal(barrier, inc=1, device_id={"seq": d}, device_id_type=MESH)
-    )
+    for offset in away:
+        for dy in (2, 1, 3, 0):
+            if offset or dy:
+                pl.semaphore_signal(
+                    barrier, inc=1, device_id_type=MESH,
+                    device_id={"seq": device(line_at(dy), pair_at(offset), side)},
+                )
+        pl.semaphore_signal(
+            barrier, inc=1, device_id_type=MESH,
+            device_id={"seq": device(line, pair_at(offset), 1 - side)},
+        )
     for i in range(1, n_head):
         pl.semaphore_signal(
             barrier, inc=1, device_id={"head": lax.rem(mine + i, n_head)}, device_id_type=MESH
@@ -125,11 +140,19 @@
         top = top + nn(nt(a[lo], b[hi]).astype(BF16), c[hi])
         return top, low
 
+    def put_state(ref, h, value):
+        first = LINES * (h % 2)
+        ref[h // 2, first : first + LINES] = value.reshape(LINES, LINES, ROWS, HEAD)
+
+    def state_of(ref, h):
+        first = LINES * (h % 2)
+        return ref[h // 2, first : first + LINES].reshape(HEAD, HEAD)
+
     loads[0].wait()
     loads[1].wait()
     for h in range(heads):
         kv = tn(k[:, cols(h)], v[:, cols(h)])
-        local1[h * PLANES : (h + 1) * PLANES] = kv.reshape(PLANES, ROWS, HEAD)
+        put_state(local1, h, kv)
     for load in loads[2:]:
         load.wait()
 
@@ -139,43 +162,101 @@
         att[hi, cols(h)] = low
 
     forward_inside(0)
-    pl.semaphore_wait(barrier, n_seq - 1 + n_head - 1)
-
-    def all_but_one(ref):
-        return ref.at[pl.ds(0, n_seq - 1)]
-
-    def scatter(local, got, sems):
-        each_seq(
-            lambda d: copy_to(
-                local.at[d], got.at[me], send_sem.at[sems], recv_sem.at[sems], seq=d
-            ).start()
-        )
-        got[me] = local[me]
-
-    def arrived(ref, sems):
-        ref = all_but_one(ref)
-        copy_to(ref, ref, send_sem.at[sems], recv_sem.at[sems], seq=me).wait_recv()
-
-    def sent(ref, sems):
-        ref = all_but_one(ref)
-        copy_to(ref, ref, send_sem.at[sems], recv_sem.at[sems], seq=me).wait_send()
-
-    scatter(local1, got1, 0)
+    pl.semaphore_wait(barrier, n_seq // 2 - 1 + pairs + n_head - 1)
+
+    class Scan:
+        def __init__(self, local, result, other, sums, got, part, back, share, index, reverse):
+            self.local, self.result, self.other, self.sums = local, result, other, sums
+            self.got, self.part, self.back, self.share = got, part, back, share
+            self.index, self.reverse = index, reverse
+
+        def copy(self, src, dst, send, recv, to):
+            return copy_to(
+                src, dst, scan_send.at[4 * self.index + send],
+                scan_recv.at[(2 * pairs + 2) * self.index + recv], seq=to,
+            )
+
+        def to_mate(self):
+            for j, offset in enumerate(away):
+                p = pair_at(offset)
+                self.copy(self.local.at[1 - side, p], self.other.at[p], 0, j, mate).start()
+
+        def to_owners(self):
+            place = line * pairs + pair
+            for j, offset in enumerate(away):
+                p = pair_at(offset)
+                chunk = self.other.at[p]
+                self.copy(chunk, chunk, 0, j, mate).wait_recv()
+                self.sums[p] = self.other[p] + self.local[side, p]
+                for dy in (2, 1, 3, 0):
+                    y = line_at(dy)
+                    if offset or dy:
+                        self.copy(
+                            self.sums.at[p, y], self.got.at[place], 1, pairs, device(y, p, side)
+                        ).start()
+                    else:
+                        self.got[place] = self.sums[p, y]
+
+        def add_up(self, total):
+            most = self.got.at[pl.ds(0, LINES * pairs - 1)]
+            self.copy(most, most, 1, pairs, mate).wait_recv()
+            order = range(LINES * pairs)
+            for b in reversed(order) if self.reverse else order:
+                self.part[b] = total
+                total = total + self.got[b]
+            return total
+
+        def to_blocks(self):
+            for offset in away:
+                p = pair_at(offset)
+                recv = pairs + 1 + (pairs - offset) % pairs
+                for dy in (2, 1, 3, 0):
+                    y = line_at(dy)
+                    part = self.part.at[y * pairs + p]
+                    if offset or dy:
+                        self.copy(
+                            part, self.back.at[pair, line], 2, recv, device(y, p, side)
+                        ).start()
+                    else:
+                        self.back[pair, line] = self.part[y * pairs + p]
+
+        def to_mate_back(self):
+            second = side == (0 if self.reverse else 1)
+            for offset in away:
+                p = pair_at(offset)
+                chunk = self.back.at[p] if offset else self.back.at[p, pl.ds(0, LINES - 1)]
+                self.copy(chunk, chunk, 2, pairs + 1 + offset, mate).wait_recv()
+                base = self.back[p]
+                self.share[p] = base + jnp.where(second, 0.0, self.local[side, p])
+                self.copy(
+                    self.share.at[p], self.result.at[side, p], 3, 2 * pairs + 1, mate
+                ).start()
+                self.result[side, p] = base + jnp.where(second, self.other[p], 0.0)
+
+        def finish(self):
+            whole = self.result.at[0]
+            self.copy(whole, whole, 3, 2 * pairs + 1, mate).wait_recv()
+
+        def sent(self):
+            whole = self.result.at[0]
+            most = self.got.at[pl.ds(0, LINES * pairs - 1)]
+            for send, ref in enumerate((whole, most, most, whole)):
+                self.copy(ref, ref, send, 0, mate).wait_send()
+
+    scan1 = Scan(local1, before, mate1, sums1, got1, part1, back1, share1, 0, False)
+    scan2 = Scan(local2, after, mate2, sums2, got2, part2, back2, share2, 1, True)
+
+    scan1.to_mate()
     forward_inside(1)
+    scan1.to_owners()
     for h in range(heads):
         qt[h] = q[:, cols(h)].T
-    arrived(got1, 0)
-    total = state_ref[me]
-    for b in range(n_seq):
-        part1[b] = total
-        total = total + got1[b]
-    scatter(part1, before, 1)
-    for h in range(2, heads):
-        forward_inside(h)
-    arrived(before, 1)
-
-    def state_of(ref, h):
-        return ref[h * PLANES : (h + 1) * PLANES].reshape(HEAD, HEAD)
+    forward_inside(2)
+    scan1.add_up(state_ref[side * (n_seq // 2) + pair * LINES + line])
+    scan1.to_blocks()
+    forward_inside(3)
+    scan1.to_mate_back()
+    scan1.finish()
 
     def gain_of(h):
         return gain_ref[h : h + 1, :]
@@ -221,8 +302,8 @@
         d_low = d.astype(BF16)
         dfull[:, cols(h)] = d
         dlow[:, cols(h)] = d_low
-        local2[h * PLANES : (h + 1) * PLANES] = nn(qt[h], d_low).reshape(PLANES, ROWS, HEAD)
-    scatter(local2, got2, 3)
+        put_state(local2, h, nn(qt[h], d_low))
+    scan2.to_mate()
 
     gains[0] = jnp.zeros((ROWS, HEAD), F32)
     for h in range(heads):
@@ -231,6 +312,8 @@
         gains[0, h : h + 1, :] = jnp.sum(
             u[:, cols(h)].astype(F32) * normed, axis=0, keepdims=True
         )
+
+    scan2.to_owners()
 
     def partner(i):
         step = (1, 2, 4, 8, 1, 2)[i]
@@ -266,12 +349,7 @@
             gain_step(0)
     gain_step(1)
 
-    arrived(got2, 3)
-    total = jnp.zeros((ROWS, HEAD), F32)
-    for b in reversed(range(n_seq)):
-        part2[b] = total
-        total = total + got2[b]
-    totals[me] = total
+    totals[me] = scan2.add_up(jnp.zeros((ROWS, HEAD), F32))
 
     def send_total(j, carry):
         copy_to(
@@ -281,7 +359,7 @@
         return carry
 
     lax.fori_loop(0, PLANES - 1, send_total, 0)
-    scatter(part2, after, 4)
+    scan2.to_blocks()
 
     for h in range(heads):
         top, low = anticausal(v[:, cols(h)], dlow[:, cols(h)], q[:, cols(h)])
@@ -291,6 +369,7 @@
         vpart[lo, cols(h)] = top
         vpart[hi, cols(h)] = low
 
+    scan2.to_mate_back()
     row = totals.at[pl.ds(line * PLANES, PLANES)]
     some = totals.at[pl.ds(0, PLANES - 1)]
     copy_to(some, some, send_sem.at[5], recv_sem.at[5], seq=me).wait_recv()
@@ -301,7 +380,7 @@
         ).start()
     gain_step(2)
 
-    arrived(after, 4)
+    scan2.finish()
     for h in range(heads):
         high, low = halves(state_of(after, h))
         vh, kh = v[:, cols(h)], k[:, cols(h)]
@@ -311,16 +390,16 @@
     gain_step(3)
     three = totals.at[pl.ds(0, (LINES - 1) * PLANES)]
     copy_to(three, three, send_sem.at[6], recv_sem.at[6], seq=me).wait_recv()
-    state_out[...] = totals[...]
+    for at in range(n_seq):
+        owner = device(at % LINES, at % (n_seq // 2) // LINES, at // (n_seq // 2))
+        state_out[at] = totals[owner]
     gain_step(4)
     gain_step(5)
     gain_out[...] = gains[6, :heads, :]
 
-    sent(local1, 0)
-    sent(part1, 1)
+    scan1.sent()
+    scan2.sent()
     copy_to(others, others, send_sem.at[2], recv_sem.at[2], head=mine).wait_send()
-    sent(local2, 3)
-    sent(part2, 4)
     copy_to(some, some, send_sem.at[5], recv_sem.at[5], seq=me).wait_send()
     copy_to(three, three, send_sem.at[6], recv_sem.at[6], seq=me).wait_send()
     for i in range(6):
@@ -348,6 +427,10 @@
     hbm = pl.BlockSpec(memory_space=pltpu.HBM)
     low = pltpu.VMEM((tokens, columns), BF16)
     full = pltpu.VMEM((tokens, columns), F32)
+    pairs = PLANES // 2
+    whole = pltpu.VMEM((2, pairs, LINES, ROWS, HEAD), F32)
+    half = pltpu.VMEM((pairs, LINES, ROWS, HEAD), F32)
+    flat = pltpu.VMEM((pairs * LINES, ROWS, HEAD), F32)
     shapes = (
         wide, wide, wide, wide,
         jax.ShapeDtypeStruct((heads, HEAD), F32),
@@ -362,7 +445,7 @@
         scratch_shapes=[low] * 4
         + [pltpu.VMEM((heads, HEAD), F32), pltpu.VMEM(slices, F32)]
         + [pltpu.VMEM((heads, HEAD, tokens), BF16), full, full, low, full, full]
-        + [pltpu.VMEM(slices, F32)] * 8
+        + ([whole] * 2 + [half] * 2 + [flat] * 2 + [half] * 2) * 2
         + [
             pltpu.VMEM((n_head, ROWS, HEAD), F32),
             pltpu.VMEM(slices, F32),
@@ -371,6 +454,8 @@
             pltpu.SemaphoreType.DMA((6,)),
             pltpu.SemaphoreType.DMA((13,)),
             pltpu.SemaphoreType.DMA((13,)),
+            pltpu.SemaphoreType.DMA((8,)),
+            pltpu.SemaphoreType.DMA((2 * (2 * pairs + 2),)),
         ],
         compiler_params=pltpu.CompilerParams(
             collective_id=0, has_side_effects=True, vmem_limit_bytes=51 << 20

time: 94.9 us -> 92.8 us (0.978)
  Pallas kernels: 92.5 us -> 90.3 us
    pallas_call x1, Pallas kernels: 91 us -> 88.9 us  [per_device(): pl.pallas_call(kernel, name='attention_and_gradients', out_shape=shapes,...]
where the time goes in v3:
time: 92.8 us; the launch traced here: 92.6 us
  Pallas kernels  90.3 us (97%)
  local copies, waits for them, and re-layouts  1.62 us (2%)
    pallas_call x1, Pallas kernels, per_device(): pl.pallas_call(kernel, name='attention_and_gradients', out_shape=shapes,...  88.9 us

profile of v3, /device:TPU:2, one launch (start us, length us, event | category | flops | bytes accessed | tf_op | source)
XLA Modules:
  0.0 92.6 jit_solution(18055028021425761527)
XLA Ops:
  0.6 0.0 copy-start.1
  0.6 0.7 copy-done.1
  1.3 0.0 copy-start
  1.3 0.9 %copy-done = f32[4,128,128]{2,1,0:T(8,128)S(1)} copy-done((f32[4,128,128]{2,1,0:T(8,128)S(1)}, f32[4,128,128]{2,1,0:T(8,128)}, u32[]{:S(2)}) %copy-start) | copy-done | bytes 262168
  2.3 88.9 %attention_and_gradients.1 = (bf16[512,512]{1,0:T(8,128)(2,1)S(1)}, bf16[512,512]{1,0:T(8,128)(2,1)S(1)}, bf16[512,512]{1,0:T(8,128)(2,1)S(1)}, bf16[512,512]{1,...) custom-call(bf16[512,512]{1,0:T(8,128)(2,1)} %q_in.1, bf16[512,512]{1,0:T(8,128)(2,1)} %k_in.1, ...), custom_call_target="tpu_custom_call" | custom-call | tf_op jit(solution)/shard_map/attention_and_gradients/pallas_call | solution.py:439
  91.1 1.5 %store.1 = (bf16[512,512]{1,0:T(8,128)(2,1)}, bf16[512,512]{1,0:T(8,128)(2,1)}, bf16[512,512]{1,0:T(8,128)(2,1)}, bf16[512,512]{1,0:T(8,128)(2,1)}, f32[4,128]{1,0:T(4,128)}, /*index=5*/f32[64,8,128]{2,1,0:T(8,128)}) custom-call(bf16[512,512]{1,0:T(8,128)(2,1)S(1)} %get-tuple-element.18.refs_0_, bf16[512,512]{1,0:T(8,128)(2,1)S(1)} %get-tuple-element.19.refs_1_, ...), custom_call_target="tpu_custom_call" | custom-call | tf_op jit(solution)/shard_map/store/pallas_call | solution.py:467
Async XLA Ops:
  0.6 0.7 copy-start.1
  1.3 0.9 %copy-start = (f32[4,128,128]{2,1,0:T(8,128)S(1)}, f32[4,128,128]{2,1,0:T(8,128)}, u32[]{:S(2)}) copy-start(f32[4,128,128]{2,1,0:T(8,128)} %param.11) | copy-start | bytes 786436

commit v4 on v3

--- a/solution.py
+++ b/solution.py
@@ -45,7 +45,7 @@
     q, k, v, u, gain_ref, state_ref, qt, att, dfull, dlow, kpart, vpart,
     local1, before, mate1, sums1, got1, part1, back1, share1,
     local2, after, mate2, sums2, got2, part2, back2, share2,
-    stats, totals, gains, gains_got,
+    stats, totals, gains, line_gains, all_gains,
     in_sem, send_sem, recv_sem, scan_send, scan_recv,
 ):
     n_seq = lax.axis_size("seq")
@@ -313,26 +313,18 @@
             u[:, cols(h)].astype(F32) * normed, axis=0, keepdims=True
         )
 
+    to_mate = copy_to(gains.at[0], gains.at[3], send_sem.at[7], recv_sem.at[7], seq=mate)
+    to_mate.start()
     scan2.to_owners()
 
-    def partner(i):
-        step = (1, 2, 4, 8, 1, 2)[i]
-        near = plane if i < 4 else line
-        other = near + step - 2 * step * lax.rem(near // step, 2)
-        return line * PLANES + other if i < 4 else other * PLANES + plane
-
-    def gain_copy(i):
-        return copy_to(
-            gains.at[i], gains_got.at[i], send_sem.at[7 + i], recv_sem.at[7 + i], seq=partner(i)
-        )
-
-    def gain_step(i):
-        gain_copy(i).wait_recv()
-        gains[i + 1] = gains[i] + gains_got[i]
-        if i < 5:
-            gain_copy(i + 1).start()
-
-    gain_copy(0).start()
+    to_mate.wait_recv()
+    gains[1] = gains[0] + gains[3]
+    line_gains[pair] = gains[1]
+    for offset in away[:-1]:
+        copy_to(
+            gains.at[1], line_gains.at[pair], send_sem.at[8], recv_sem.at[8],
+            seq=device(line, pair_at(offset), side),
+        ).start()
 
     def query_gradient(h):
         d_low = dlow[:, cols(h)]
@@ -345,9 +337,6 @@
 
     for h in range(heads):
         query_gradient(h)
-        if h == 1:
-            gain_step(0)
-    gain_step(1)
 
     totals[me] = scan2.add_up(jnp.zeros((ROWS, HEAD), F32))
 
@@ -369,41 +358,60 @@
         vpart[lo, cols(h)] = top
         vpart[hi, cols(h)] = low
 
-    scan2.to_mate_back()
-    row = totals.at[pl.ds(line * PLANES, PLANES)]
     some = totals.at[pl.ds(0, PLANES - 1)]
     copy_to(some, some, send_sem.at[5], recv_sem.at[5], seq=me).wait_recv()
+    row = totals.at[pl.ds(line * PLANES, PLANES)]
     for i in (2, 1, 3):
         copy_to(
-            row, row, send_sem.at[6], recv_sem.at[6],
-            seq=lax.rem(line + i, LINES) * PLANES + plane,
+            row, row, send_sem.at[6], recv_sem.at[6], seq=device(line_at(i), pair, side)
         ).start()
-    gain_step(2)
-
+    seven = line_gains.at[pl.ds(0, pairs - 1)]
+    copy_to(seven, seven, send_sem.at[8], recv_sem.at[8], seq=me).wait_recv()
+    gain = line_gains[0]
+    for i in range(1, pairs):
+        gain = gain + line_gains[i]
+    gains[2] = gain
+    all_gains[line] = gain
+    for i in (2, 1, 3):
+        copy_to(
+            gains.at[2], all_gains.at[line], send_sem.at[9], recv_sem.at[9],
+            seq=device(line_at(i), pair, side),
+        ).start()
+
+    def other_gradients(part):
+        for i in range(heads // 2):
+            at = pl.ds(pl.multiple_of((heads // 2 * part + i) * HEAD, HEAD), HEAD)
+            rows_i = after[part, LINES * i : LINES * (i + 1)].reshape(HEAD, HEAD)
+            high, low = halves(rows_i)
+            vh, kh = v[:, at], k[:, at]
+            kgrad_out[:, at] = (kpart[:, at] + (nt(vh, high) + nt(vh, low))).astype(BF16)
+            vgrad_out[:, at] = (vpart[:, at] + (nn(kh, high) + nn(kh, low))).astype(BF16)
+
+    scan2.to_mate_back()
+    other_gradients(side)
     scan2.finish()
-    for h in range(heads):
-        high, low = halves(state_of(after, h))
-        vh, kh = v[:, cols(h)], k[:, cols(h)]
-        kgrad_out[:, cols(h)] = (kpart[:, cols(h)] + (nt(vh, high) + nt(vh, low))).astype(BF16)
-        vgrad_out[:, cols(h)] = (vpart[:, cols(h)] + (nn(kh, high) + nn(kh, low))).astype(BF16)
-
-    gain_step(3)
+    other_gradients(1 - side)
+
     three = totals.at[pl.ds(0, (LINES - 1) * PLANES)]
     copy_to(three, three, send_sem.at[6], recv_sem.at[6], seq=me).wait_recv()
     for at in range(n_seq):
         owner = device(at % LINES, at % (n_seq // 2) // LINES, at // (n_seq // 2))
         state_out[at] = totals[owner]
-    gain_step(4)
-    gain_step(5)
-    gain_out[...] = gains[6, :heads, :]
+    some_gains = all_gains.at[pl.ds(0, LINES - 1)]
+    copy_to(some_gains, some_gains, send_sem.at[9], recv_sem.at[9], seq=me).wait_recv()
+    gain = all_gains[0]
+    for i in range(1, LINES):
+        gain = gain + all_gains[i]
+    gain_out[...] = gain[:heads]
 
     scan1.sent()
     scan2.sent()
     copy_to(others, others, send_sem.at[2], recv_sem.at[2], head=mine).wait_send()
     copy_to(some, some, send_sem.at[5], recv_sem.at[5], seq=me).wait_send()
     copy_to(three, three, send_sem.at[6], recv_sem.at[6], seq=me).wait_send()
-    for i in range(6):
-        gain_copy(i).wait_send()
+    to_mate.wait_send()
+    copy_to(seven, seven, send_sem.at[8], recv_sem.at[8], seq=me).wait_send()
+    copy_to(some_gains, some_gains, send_sem.at[9], recv_sem.at[9], seq=me).wait_send()
 
 
 def store_kernel(*refs):
@@ -449,11 +457,12 @@
         + [
             pltpu.VMEM((n_head, ROWS, HEAD), F32),
             pltpu.VMEM(slices, F32),
-            pltpu.VMEM((7, ROWS, HEAD), F32),
-            pltpu.VMEM((6, ROWS, HEAD), F32),
+            pltpu.VMEM((4, ROWS, HEAD), F32),
+            pltpu.VMEM((pairs, ROWS, HEAD), F32),
+            pltpu.VMEM((LINES, ROWS, HEAD), F32),
             pltpu.SemaphoreType.DMA((6,)),
-            pltpu.SemaphoreType.DMA((13,)),
-            pltpu.SemaphoreType.DMA((13,)),
+            pltpu.SemaphoreType.DMA((10,)),
+            pltpu.SemaphoreType.DMA((10,)),
             pltpu.SemaphoreType.DMA((8,)),
             pltpu.SemaphoreType.DMA((2 * (2 * pairs + 2),)),
         ],

time: 92.8 us -> 82.2 us (0.89)
  the two profiles are of different devices: /device:TPU:2 before, /device:TPU:8 now
where the time goes in v4:
time: 82.2 us; the launch traced here: 82 us
  Pallas kernels  79.7 us (97%)
  local copies, waits for them, and re-layouts  1.62 us (2%)
    pallas_call x1, Pallas kernels, per_device(): pl.pallas_call(kernel, name='attention_and_gradients', out_shape=shapes,...  78.3 us

profile of v4, /device:TPU:8, one launch (start us, length us, event | category | flops | bytes accessed | tf_op | source)
XLA Modules:
  0.0 82.0 jit_solution(4918108464185016300)
XLA Ops:
  0.6 0.0 copy-start.1
  0.6 0.7 copy-done.1
  1.3 0.0 copy-start
  1.3 0.9 %copy-done = f32[4,128,128]{2,1,0:T(8,128)S(1)} copy-done((f32[4,128,128]{2,1,0:T(8,128)S(1)}, f32[4,128,128]{2,1,0:T(8,128)}, u32[]{:S(2)}) %copy-start) | copy-done | bytes 262168
  2.3 78.3 %attention_and_gradients.1 = (bf16[512,512]{1,0:T(8,128)(2,1)S(1)}, bf16[512,512]{1,0:T(8,128)(2,1)S(1)}, bf16[512,512]{1,0:T(8,128)(2,1)S(1)}, bf16[512,512]{1,...) custom-call(bf16[512,512]{1,0:T(8,128)(2,1)} %q_in.1, bf16[512,512]{1,0:T(8,128)(2,1)} %k_in.1, ...), custom_call_target="tpu_custom_call" | custom-call | tf_op jit(solution)/shard_map/attention_and_gradients/pallas_call | solution.py:447
  80.6 1.5 %store.1 = (bf16[512,512]{1,0:T(8,128)(2,1)}, bf16[512,512]{1,0:T(8,128)(2,1)}, bf16[512,512]{1,0:T(8,128)(2,1)}, bf16[512,512]{1,0:T(8,128)(2,1)}, f32[4,128]{1,0:T(4,128)}, /*index=5*/f32[64,8,128]{2,1,0:T(8,128)}) custom-call(bf16[512,512]{1,0:T(8,128)(2,1)S(1)} %get-tuple-element.18.refs_0_, bf16[512,512]{1,0:T(8,128)(2,1)S(1)} %get-tuple-element.19.refs_1_, ...), custom_call_target="tpu_custom_call" | custom-call | tf_op jit(solution)/shard_map/store/pallas_call | solution.py:476
Async XLA Ops:
  0.6 0.7 copy-start.1
  1.3 0.9 %copy-start = (f32[4,128,128]{2,1,0:T(8,128)S(1)}, f32[4,128,128]{2,1,0:T(8,128)}, u32[]{:S(2)}) copy-start(f32[4,128,128]{2,1,0:T(8,128)} %param.11) | copy-start | bytes 786436

commit v5 on v4

--- a/solution.py
+++ b/solution.py
@@ -222,7 +222,7 @@
 
         def to_mate_back(self):
             second = side == (0 if self.reverse else 1)
-            for offset in away:
+            for offset in reversed(away):
                 p = pair_at(offset)
                 chunk = self.back.at[p] if offset else self.back.at[p, pl.ds(0, LINES - 1)]
                 self.copy(chunk, chunk, 2, pairs + 1 + offset, mate).wait_recv()
@@ -256,20 +256,25 @@
     scan1.to_blocks()
     forward_inside(3)
     scan1.to_mate_back()
-    scan1.finish()
 
     def gain_of(h):
         return gain_ref[h : h + 1, :]
 
-    squares = jnp.zeros((tokens, HEAD), F32)
-    products = jnp.zeros((tokens, HEAD), F32)
-    for h in range(heads):
-        high, low = halves(state_of(before, h))
-        qh = q[:, cols(h)]
-        a = att[:, cols(h)] + (nn(qh, high) + nn(qh, low))
-        att[:, cols(h)] = a
-        squares = squares + a * a
-        products = products + a * (u[:, cols(h)].astype(F32) * gain_of(h))
+    def forward_carried(part, squares, products):
+        for i in range(heads // 2):
+            h = heads // 2 * part + i
+            at = pl.ds(pl.multiple_of(h * HEAD, HEAD), HEAD)
+            high, low = halves(before[part, LINES * i : LINES * (i + 1)].reshape(HEAD, HEAD))
+            a = att[:, at] + (nn(q[:, at], high) + nn(q[:, at], low))
+            att[:, at] = a
+            squares = squares + a * a
+            products = products + a * (u[:, at].astype(F32) * gain_ref[pl.ds(h, 1), :])
+        return squares, products
+
+    nothing = jnp.zeros((tokens, HEAD), F32)
+    squares, products = forward_carried(side, nothing, nothing)
+    scan1.finish()
+    squares, products = forward_carried(1 - side, squares, products)
     blocks = tokens // HEAD
     for j in range(blocks):
         rows_j = slice(j * HEAD, (j + 1) * HEAD)
@@ -416,7 +421,17 @@
 
 def store_kernel(*refs):
     n = len(refs) // 2
-    stores = [pltpu.make_async_copy(refs[i], refs[n + i], refs[-1].at[i]) for i in range(n)]
+    stores = []
+    for i in range(n):
+        cuts = 4 if i < 4 else 1
+        rows = refs[i].shape[0] // cuts
+        for c in range(cuts):
+            at = pl.ds(c * rows, rows)
+            stores.append(
+                pltpu.make_async_copy(
+                    refs[i].at[at], refs[n + i].at[at], refs[-1].at[len(stores)]
+                )
+            )
     for store in stores:
         store.start()
     for store in stores:
@@ -479,7 +494,7 @@
         out_shape=shapes,
         in_specs=[anywhere] * 6,
         out_specs=[hbm] * 6,
-        scratch_shapes=[pltpu.SemaphoreType.DMA((6,))],
+        scratch_shapes=[pltpu.SemaphoreType.DMA((18,))],
         compiler_params=pltpu.CompilerParams(vmem_limit_bytes=1 << 20),
     )(*outs)
     return (

time: 82.2 us -> 79.8 us (0.971)
  Pallas kernels: 79.7 us -> 77.3 us
    pallas_call x1, Pallas kernels: 78.3 us -> 75.7 us  [per_device(): pl.pallas_call(kernel, name='attention_and_gradients', out_shape=shapes,...]
where the time goes in v5:
time: 79.8 us; the launch traced here: 79.6 us
  Pallas kernels  77.3 us (97%)
  local copies, waits for them, and re-layouts  1.62 us (2%)
    pallas_call x1, Pallas kernels, per_device(): pl.pallas_call(kernel, name='attention_and_gradients', out_shape=shapes,...  75.7 us
    unnamed x4, local copies, waits for them, and re-layouts  1.62 us

profile of v5, /device:TPU:8, one launch (start us, length us, event | category | flops | bytes accessed | tf_op | source)
XLA Modules:
  0.0 79.6 jit_solution(11423879619765614429)
XLA Ops:
  0.6 0.0 copy-start.1
  0.6 0.7 copy-done.1
  1.3 0.0 copy-start
  1.3 0.9 %copy-done = f32[4,128,128]{2,1,0:T(8,128)S(1)} copy-done((f32[4,128,128]{2,1,0:T(8,128)S(1)}, f32[4,128,128]{2,1,0:T(8,128)}, u32[]{:S(2)}) %copy-start) | copy-done | bytes 262168
  2.3 75.7 %attention_and_gradients.1 = (bf16[512,512]{1,0:T(8,128)(2,1)S(1)}, bf16[512,512]{1,0:T(8,128)(2,1)S(1)}, bf16[512,512]{1,0:T(8,128)(2,1)S(1)}, bf16[512,512]{1,...) custom-call(bf16[512,512]{1,0:T(8,128)(2,1)} %q_in.1, bf16[512,512]{1,0:T(8,128)(2,1)} %k_in.1, ...), custom_call_target="tpu_custom_call" | custom-call | tf_op jit(solution)/shard_map/attention_and_gradients/pallas_call | solution.py:462
  78.0 1.6 %store.1 = (bf16[512,512]{1,0:T(8,128)(2,1)}, bf16[512,512]{1,0:T(8,128)(2,1)}, bf16[512,512]{1,0:T(8,128)(2,1)}, bf16[512,512]{1,0:T(8,128)(2,1)}, f32[4,128]{1,0:T(4,128)}, /*index=5*/f32[64,8,128]{2,1,0:T(8,128)}) custom-call(bf16[512,512]{1,0:T(8,128)(2,1)S(1)} %get-tuple-element.18.refs_0_, bf16[512,512]{1,0:T(8,128)(2,1)S(1)} %get-tuple-element.19.refs_1_, ...), custom_call_target="tpu_custom_call" | custom-call | tf_op jit(solution)/shard_map/store/pallas_call | solution.py:491
Async XLA Ops:
  0.6 0.7 copy-start.1
  1.3 0.9 %copy-start = (f32[4,128,128]{2,1,0:T(8,128)S(1)}, f32[4,128,128]{2,1,0:T(8,128)}, u32[]{:S(2)}) copy-start(f32[4,128,128]{2,1,0:T(8,128)} %param.11) | copy-start | bytes 786436

commit v6 on v5

--- a/solution.py
+++ b/solution.py
@@ -423,7 +423,7 @@
     n = len(refs) // 2
     stores = []
     for i in range(n):
-        cuts = 4 if i < 4 else 1
+        cuts = 1
         rows = refs[i].shape[0] // cuts
         for c in range(cuts):
             at = pl.ds(c * rows, rows)
@@ -485,8 +485,13 @@
             collective_id=0, has_side_effects=True, vmem_limit_bytes=51 << 20
         ),
     )(
-        query_in, key_in, value_in, upstream,
-        norm_gain.reshape(heads, HEAD), state_in.reshape(slices),
+        *(
+            pltpu.with_memory_space_constraint(x, pltpu.HBM)
+            for x in (
+                query_in, key_in, value_in, upstream,
+                norm_gain.reshape(heads, HEAD), state_in.reshape(slices),
+            )
+        )
     )
     outs = pl.pallas_call(
         store_kernel,
@@ -494,7 +499,7 @@
         out_shape=shapes,
         in_specs=[anywhere] * 6,
         out_specs=[hbm] * 6,
-        scratch_shapes=[pltpu.SemaphoreType.DMA((18,))],
+        scratch_shapes=[pltpu.SemaphoreType.DMA((6,))],
         compiler_params=pltpu.CompilerParams(vmem_limit_bytes=1 << 20),
     )(*outs)
     return (

time: 79.8 us -> 77.9 us (0.976)
  local copies, waits for them, and re-layouts: 1.62 us -> 0 us
    unnamed x4 -> x0, local copies, waits for them, and re-layouts: 1.62 us -> none
where the time goes in v6:
time: 77.9 us; the launch traced here: 77.8 us
  Pallas kernels  77.1 us (99%)
    pallas_call x1, Pallas kernels, per_device(): pl.pallas_call(kernel, name='attention_and_gradients', out_shape=shapes,...  75.7 us

profile of v6, /device:TPU:8, one launch (start us, length us, event | category | flops | bytes accessed | tf_op | source)
XLA Modules:
  0.0 77.8 jit_solution(10151233522851236716)
XLA Ops:
  0.6 75.7 %attention_and_gradients.1 = (bf16[512,512]{1,0:T(8,128)(2,1)S(1)}, bf16[512,512]{1,0:T(8,128)(2,1)S(1)}, bf16[512,512]{1,0:T(8,128)(2,1)S(1)}, bf16[512,512]{1,...) custom-call(bf16[512,512]{1,0:T(8,128)(2,1)} %q_in.1, bf16[512,512]{1,0:T(8,128)(2,1)} %k_in.1, ...), custom_call_target="tpu_custom_call" | custom-call | tf_op jit(solution)/shard_map/attention_and_gradients/pallas_call | solution.py:462
  76.3 1.5 %store.1 = (bf16[512,512]{1,0:T(8,128)(2,1)}, bf16[512,512]{1,0:T(8,128)(2,1)}, bf16[512,512]{1,0:T(8,128)(2,1)}, bf16[512,512]{1,0:T(8,128)(2,1)}, f32[4,128]{1,0:T(4,128)}, /*index=5*/f32[64,8,128]{2,1,0:T(8,128)}) custom-call(bf16[512,512]{1,0:T(8,128)(2,1)S(1)} %get-tuple-element.18.refs_0_, bf16[512,512]{1,0:T(8,128)(2,1)S(1)} %get-tuple-element.19.refs_1_, ...), custom_call_target="tpu_custom_call" | custom-call | tf_op jit(solution)/shard_map/store/pallas_call | solution.py:496

commit v7 on v6

--- a/solution.py
+++ b/solution.py
@@ -220,9 +220,9 @@
                     else:
                         self.back[pair, line] = self.part[y * pairs + p]
 
-        def to_mate_back(self):
+        def to_mate_back(self, offsets):
             second = side == (0 if self.reverse else 1)
-            for offset in reversed(away):
+            for offset in offsets:
                 p = pair_at(offset)
                 chunk = self.back.at[p] if offset else self.back.at[p, pl.ds(0, LINES - 1)]
                 self.copy(chunk, chunk, 2, pairs + 1 + offset, mate).wait_recv()
@@ -255,7 +255,7 @@
     scan1.add_up(state_ref[side * (n_seq // 2) + pair * LINES + line])
     scan1.to_blocks()
     forward_inside(3)
-    scan1.to_mate_back()
+    scan1.to_mate_back(away[::-1])
 
     def gain_of(h):
         return gain_ref[h : h + 1, :]
@@ -363,6 +363,7 @@
         vpart[lo, cols(h)] = top
         vpart[hi, cols(h)] = low
 
+    scan2.to_mate_back(away[pairs // 2 :][::-1])
     some = totals.at[pl.ds(0, PLANES - 1)]
     copy_to(some, some, send_sem.at[5], recv_sem.at[5], seq=me).wait_recv()
     row = totals.at[pl.ds(line * PLANES, PLANES)]
@@ -392,7 +393,7 @@
             kgrad_out[:, at] = (kpart[:, at] + (nt(vh, high) + nt(vh, low))).astype(BF16)
             vgrad_out[:, at] = (vpart[:, at] + (nn(kh, high) + nn(kh, low))).astype(BF16)
 
-    scan2.to_mate_back()
+    scan2.to_mate_back(away[: pairs // 2][::-1])
     other_gradients(side)
     scan2.finish()
     other_gradients(1 - side)

time: 77.9 us -> 78.1 us (level)
  no operation moved by 1% of the time
where the time goes in v7:
time: 78.1 us; the launch traced here: 78 us
  Pallas kernels  77.3 us (99%)
    pallas_call x1, Pallas kernels, per_device(): pl.pallas_call(kernel, name='attention_and_gradients', out_shape=shapes,...  75.9 us

profile of v7, /device:TPU:8, one launch (start us, length us, event | category | flops | bytes accessed | tf_op | source)
XLA Modules:
  0.0 78.0 jit_solution(169037719237746309)
XLA Ops:
  0.6 75.9 %attention_and_gradients.1 = (bf16[512,512]{1,0:T(8,128)(2,1)S(1)}, bf16[512,512]{1,0:T(8,128)(2,1)S(1)}, bf16[512,512]{1,0:T(8,128)(2,1)S(1)}, bf16[512,512]{1,...) custom-call(bf16[512,512]{1,0:T(8,128)(2,1)} %q_in.1, bf16[512,512]{1,0:T(8,128)(2,1)} %k_in.1, ...), custom_call_target="tpu_custom_call" | custom-call | tf_op jit(solution)/shard_map/attention_and_gradients/pallas_call | solution.py:463
  76.5 1.5 %store.1 = (bf16[512,512]{1,0:T(8,128)(2,1)}, bf16[512,512]{1,0:T(8,128)(2,1)}, bf16[512,512]{1,0:T(8,128)(2,1)}, bf16[512,512]{1,0:T(8,128)(2,1)}, f32[4,128]{1,0:T(4,128)}, /*index=5*/f32[64,8,128]{2,1,0:T(8,128)}) custom-call(bf16[512,512]{1,0:T(8,128)(2,1)S(1)} %get-tuple-element.18.refs_0_, bf16[512,512]{1,0:T(8,128)(2,1)S(1)} %get-tuple-element.19.refs_1_, ...), custom_call_target="tpu_custom_call" | custom-call | tf_op jit(solution)/shard_map/store/pallas_call | solution.py:497

commit v8 on v7

--- a/solution.py
+++ b/solution.py
@@ -352,8 +352,8 @@
         ).start()
         return carry
 
+    scan2.to_blocks()
     lax.fori_loop(0, PLANES - 1, send_total, 0)
-    scan2.to_blocks()
 
     for h in range(heads):
         top, low = anticausal(v[:, cols(h)], dlow[:, cols(h)], q[:, cols(h)])

time: 78.1 us -> 80.2 us (1.027)
  the two profiles are of different devices: /device:TPU:8 before, /device:TPU:32 now
where the time goes in v8:
time: 80.2 us; the launch traced here: 80.1 us
  Pallas kernels  79.4 us (99%)
    pallas_call x1, Pallas kernels, per_device(): pl.pallas_call(kernel, name='attention_and_gradients', out_shape=shapes,...  78 us

profile of v8, /device:TPU:32, one launch (start us, length us, event | category | flops | bytes accessed | tf_op | source)
XLA Modules:
  0.0 80.1 jit_solution(4052543074496974879)
XLA Ops:
  0.6 78.0 %attention_and_gradients.1 = (bf16[512,512]{1,0:T(8,128)(2,1)S(1)}, bf16[512,512]{1,0:T(8,128)(2,1)S(1)}, bf16[512,512]{1,0:T(8,128)(2,1)S(1)}, bf16[512,512]{1,...) custom-call(bf16[512,512]{1,0:T(8,128)(2,1)} %q_in.1, bf16[512,512]{1,0:T(8,128)(2,1)} %k_in.1, ...), custom_call_target="tpu_custom_call" | custom-call | tf_op jit(solution)/shard_map/attention_and_gradients/pallas_call | solution.py:463
  78.6 1.5 %store.1 = (bf16[512,512]{1,0:T(8,128)(2,1)}, bf16[512,512]{1,0:T(8,128)(2,1)}, bf16[512,512]{1,0:T(8,128)(2,1)}, bf16[512,512]{1,0:T(8,128)(2,1)}, f32[4,128]{1,0:T(4,128)}, /*index=5*/f32[64,8,128]{2,1,0:T(8,128)}) custom-call(bf16[512,512]{1,0:T(8,128)(2,1)S(1)} %get-tuple-element.18.refs_0_, bf16[512,512]{1,0:T(8,128)(2,1)S(1)} %get-tuple-element.19.refs_1_, ...), custom_call_target="tpu_custom_call" | custom-call | tf_op jit(solution)/shard_map/store/pallas_call | solution.py:497
